TPU v7x, 256 devices: a whole 4x4x8 slice. The times are simulated.
256 devices in a mesh: hid: 8 (over y, core), voc: 32 (over x, z).
Axes of the slice: x: 4, y: 4, z: 8, core: 2. Of those that a mesh axis runs over, the one named last changes fastest.
Arguments:
- hidden: bfloat16 [1024, 7168], P(None, 'hid'), may hold values from -310 to 310
- target: bfloat16 [1024, 64640], P(None, 'voc'), may hold values from -30 to 360
- head: bfloat16 [7168, 64640], P('hid', 'voc'), may hold values from -0.0625 to 0.0625
- cotangent: float32 [1024], replicated, may hold values from 30 to 300
Outputs:
- hidden_grad: bfloat16 [1024, 7168], P('voc', 'hid')
- head_grad: bfloat16 [7168, 64640], P('hid', 'voc')
- divergence: float32 [1024], P('hid')
All inputs are finite; a program needn't handle non-finite values.
Results may differ from a plain program's by a relative error of at most 0.0057.
Values may be sent and summed in bfloat16 or wider, within the bound.
A program may use at most 128 MiB of HBM per device.

v0:
```python
import jax
import jax.numpy as jnp
from jax import lax
from jax.sharding import PartitionSpec as P


def softmax_grad(draft, target, cotangent):
    logits_t = target.astype(jnp.float32)
    peak_d = jnp.max(draft, axis=-1)
    peak_t = jnp.max(logits_t, axis=-1)
    peak_d, peak_t = lax.pmax((peak_d, peak_t), "voc")
    exp_d = jnp.exp(draft - peak_d[:, None])
    exp_t = jnp.exp(logits_t - peak_t[:, None])
    sum_d, sum_t, numer = lax.psum(
        (
            jnp.sum(exp_d, axis=-1),
            jnp.sum(exp_t, axis=-1),
            jnp.sum(exp_t * (logits_t - draft), axis=-1),
        ),
        "voc",
    )
    norm_d = peak_d + jnp.log(sum_d)
    norm_t = peak_t + jnp.log(sum_t)
    probs_q = jnp.exp(draft - norm_d[:, None])
    probs_p = jnp.exp(logits_t - norm_t[:, None])
    divergence = numer / sum_t + norm_d - norm_t
    grad = (cotangent[:, None] * (probs_q - probs_p)).astype(jnp.bfloat16)
    return (grad, divergence)


def per_device(hidden, target, head, cotangent):
    rows = hidden.shape[0]
    share = rows // lax.axis_size("hid")
    offset = lax.axis_index("hid") * share
    partial_logits = jnp.dot(hidden, head, preferred_element_type=jnp.float32)
    draft = lax.psum(partial_logits, "hid")
    grad_all, divergence_all = softmax_grad(draft, target, cotangent)
    divergence = lax.dynamic_slice_in_dim(divergence_all, offset, share, 0)
    head_grad = lax.dot_general(
        hidden, grad_all, (((0,), (0,)), ((), ())), preferred_element_type=jnp.float32
    ).astype(jnp.bfloat16)
    hidden_grad = lax.psum_scatter(
        lax.dot_general(
            grad_all, head, (((1,), (1,)), ((), ())), preferred_element_type=jnp.float32
        ),
        "voc",
        scatter_dimension=0,
        tiled=True,
    ).astype(jnp.bfloat16)
    return (hidden_grad, head_grad, divergence)


def solution(mesh):
    placed = (P(None, "hid"), P(None, "voc"), P("hid", "voc"), P())
    return jax.shard_map(
        per_device,
        mesh=mesh,
        in_specs=placed,
        out_specs=(P("voc", "hid"), P("hid", "voc"), P("hid")),
        check_vma=False,
    )
```

profile of v0, /device:TPU:1, one launch (start us, length us, event | category | flops | bytes accessed | tf_op | source)
XLA Modules:
  0.0 583.8 jit_solution(14383775876127486970)
XLA Ops:
  7.2 0.0 copy-start
  7.2 0.0 all-reduce.4.cloned.1.call-start
  7.2 1.4 copy-done
  8.7 8.7 %fusion.8 = f32[1024,2020]{0,1:T(8,128)} fusion(bf16[1024,896]{1,0:T(8,128)(2,1)S(1)} %copy-done, bf16[896,2020]{0,1:T(8,128)(2,1)} %param.6), kind=kOutput, calls=%fused_computation.16 | convolution fusion | flops 3706716160 | bytes 13728768 | tf_op jit(solution)/shard_map/dot_general | solution.py:35
  17.4 0.0 all-reduce.4.cloned.1.call-update
  17.4 0.0 reduce-scatter.2.cloned.1.call-start
  17.5 2.9 reduce_max.24
  20.4 108.8 %all-reduce.4.cloned.1.call-done = f32[1024,2020]{0,1:T(8,128)} async-done(((f32[1024,2020]{0,1:T(8,128)}), f32[1024,2020]{0,1:T(8,128)}) %all-reduce.4.cloned.1.call-update) | async-done | bytes 8273936 | tf_op jit(solution)/shard_map/psum | solution.py:36
  129.2 3.9 reduce_max.23
  133.0 62.1 %all-reduce.1 = (f32[1024]{0:T(1024)S(1)}, f32[1024]{0:T(1024)S(1)}) all-reduce(bf16[1024]{0:T(1024)(128)(2,1)S(1)} %reduce_max.24, f32[1024]{0:T(1024)S(1)} %reduce_max.23), channel_id=1, replica_groups=mesh['hid'=8,'voc'=32] {'voc'}, use_global_device_ids=true, to_apply=%region_6.0 | all-reduce | flops 2048 | bytes 14336 | tf_op jit(solution)/shard_map/pmax | solution.py:11
  195.1 0.0 copy-start.2
  195.1 6.2 %fusion.3 = (f32[1024]{0:T(1024)S(1)}, f32[1024]{0:T(1024)S(1)}, f32[1024]{0:T(1024)S(1)}) fusion(bf16[1024,2020]{0,1:T(8,128)(2,1)} %param.5, f32[1024,2020]{0,1:T(8,128)} %all-reduce.4.cloned.1.call-done, f32[1024]{0:T(1024)S(1)} %get-tuple-element.9, f32[1024]{0:T(1024)S(1)} %get-tuple-element.10), kind=kLoop, calls=%fused_computation.6 | loop fusion | flops 16544768 | bytes 12431360 | tf_op jit(solution)/shard_map/reduce_sum | solution.py:18
  201.4 110.1 %all-reduce = (f32[1024]{0:T(1024)S(1)}, f32[1024]{0:T(1024)S(1)}, f32[1024]{0:T(1024)S(1)}) all-reduce(f32[1024]{0:T(1024)S(1)} %get-tuple-element.5, f32[1024]{0:T(1024)S(1)} %get-tuple-element.4, f32[1024]{0:T(1024)S(1)} %get-tuple-element.3), channel_id=1, replica_groups=mesh['hid'=8,'voc'=32] {'voc'}, use_global_device_ids=true, to_apply=%region_8.0 | all-reduce | flops 3072 | bytes 24576 | tf_op jit(solution)/shard_map/psum | solution.py:14
  311.5 0.0 copy-done.2
  311.5 0.0 copy-start.3
  311.5 6.0 %fusion.7 = bf16[1024,2020]{0,1:T(8,128)(2,1)S(1)} fusion(bf16[1024,2020]{0,1:T(8,128)(2,1)} %param.5, f32[1024,2020]{0,1:T(8,128)} %all-reduce.4.cloned.1.call-done, f32[1024]{0:T(1024)S(1)} %get-tuple-element.13, f32[1024]{0:T(1024)S(1)} %get-tuple-element.12, f32[1024]{0:T(1024)S(1)} %copy-done.2), kind=kLoop, calls=%fused_computation.10 | loop fusion | flops 12410880 | bytes 16560128 | tf_op jit(solution)/shard_map/convert_element_type | solution.py:27
  317.5 0.0 copy-start.1
  317.6 1.9 copy-done.1
  319.5 6.6 %fusion.9 = f32[1024,896]{1,0:T(8,128)} fusion(bf16[1024,2020]{0,1:T(8,128)(2,1)S(1)} %fusion.7, bf16[896,2020]{0,1:T(8,128)(2,1)S(1)} %copy-done.3), kind=kOutput, calls=%fused_computation.17 | convolution fusion | flops 3706716160 | bytes 11426816 | tf_op jit(solution)/shard_map/dot_general | solution.py:43
  326.0 0.0 reduce-scatter.2.cloned.1.call-update
  326.1 0.6 dynamic_slice.3
  326.7 8.0 %convert_bitcast_fusion = bf16[896,2020]{0,1:T(8,128)(2,1)} fusion(bf16[1024,2020]{0,1:T(8,128)(2,1)} %copy-done.1, bf16[1024,896]{1,0:T(8,128)(2,1)S(1)} %copy-done), kind=kOutput, calls=%fused_computation.12 | convolution fusion | flops 3708526080 | bytes 9591808 | tf_op jit(solution)/shard_map/dot_general | solution.py:39
  334.7 240.8 %reduce-scatter.2.cloned.1.call-done = f32[32,896]{1,0:T(8,128)} async-done(((f32[1024,896]{1,0:T(8,128)}), f32[32,896]{1,0:T(8,128)}) %reduce-scatter.2.cloned.1.call-update) | async-done | bytes 114704 | tf_op jit(solution)/shard_map/reduce_scatter | solution.py:42
  575.5 1.5 convert_element_type.17
  (2 shorter events, 0.0 us)
Async XLA Ops:
  7.2 1.5 copy-start
  7.2 122.0 %all-reduce.4.cloned.1.call-start = ((), (), s32[]{:S(2)}) async-start(), calls=%async_computation.1 | async-start | bytes 16580608 | tf_op jit(solution)/shard_map/psum | solution.py:36
  17.4 558.0 %reduce-scatter.2.cloned.1.call-start = ((), (), s32[]{:S(2)}) async-start(), calls=%async_computation.2 | async-start | bytes 3784704 | tf_op jit(solution)/shard_map/reduce_scatter | solution.py:42
  195.1 116.4 %copy-start.2 = (f32[1024]{0:T(1024)S(1)}, f32[1024]{0:T(1024)}, u32[]{:S(2)}) copy-start(f32[1024]{0:T(1024)} %param.7) | copy-start | bytes 12292
  311.5 8.0 %copy-start.3 = (bf16[896,2020]{0,1:T(8,128)(2,1)S(1)}, bf16[896,2020]{0,1:T(8,128)(2,1)}, u32[]{:S(2)}) copy-start(bf16[896,2020]{0,1:T(8,128)(2,1)} %param.6) | copy-start | bytes 10859524
  317.5 1.9 copy-start.1
Sparse Core Ops, SparseCore 0:
  17.6 111.5 all-reduce.3
  326.2 249.2 reduce-scatter.1
where the time goes:
time: 588 us; the launch traced here: 584 us
  waiting for transfers between devices  350 us (60%)
  blocking collectives  172 us (29%)
  matrix products  23.3 us (4%)
  other arithmetic  20.6 us (4%)
  between operations  14.1 us (2%)
    reduce_scatter x1, waiting for transfers between devices, per_device(): lax.psum_scatter(lax.dot_general(grad_all, head, (((1,), (1,)), ((), ()))...  241 us
    psum x1, blocking collectives, softmax_grad(): lax.psum((jnp.sum(exp_d, axis=-1), jnp.sum(exp_t, axis=-1), jnp.sum(exp_t...  110 us
    psum x1, waiting for transfers between devices, per_device(): draft = lax.psum(partial_logits, 'hid')  109 us
    pmax x1, blocking collectives, softmax_grad(): peak_d, peak_t = lax.pmax((peak_d, peak_t), 'voc')  62.1 us
  transfers between devices with their start and end apart: 2, of which 2 were waited for; matrix products, arithmetic and copies ran while one was open for 2% of the time, Pallas kernels for 0%

commit v1 on v0

v1 whole, which is shorter than its diff:
```python
import jax
import jax.numpy as jnp
from jax import lax
from jax.experimental import pallas as pl
from jax.experimental.pallas import tpu as pltpu
from jax.sharding import PartitionSpec as P

MESH = pl.DeviceIdType.MESH
F32, BF16 = jnp.float32, jnp.bfloat16
CHUNKS = ((0,), (2, 4), (6, 1), (3, 5), (7,))
N = len(CHUNKS)
SIZE = [16 * len(groups) for groups in CHUNKS]
BASE = [sum(SIZE[:c]) for c in range(N)]
WIDE = 256
ORDER = (
    "M0", "M1", "A0", "A1", "T0", "M2", "B0", "B1", "A2", "L0", "X0", "M3", "L1", "B2", "G0", "M4", "X1", "A3",
    "L2", "F0", "X2", "G1", "H0", "B3", "K0", "F1", "G2", "L3", "R0", "H1", "A4", "K1", "X3", "F2", "Z0", "B4",
    "G3", "H2", "R1", "L4", "K2", "X4", "F3", "Z1", "R2", "H3", "G4", "K3", "F4", "Z2", "R3", "H4", "O1", "K4",
    "Z3", "O0", "R4", "O2", "Z4", "W2", "W1", "W3", "O3", "W0", "O4",
)


def place(*refs):
    sem = refs[-1]
    copies = []
    for src, dst in zip(refs[:3], refs[3:6]):
        step = -(-src.shape[0] // 64) * 16
        for i in range(0, src.shape[0], step):
            span = pl.ds(i, min(step, src.shape[0] - i))
            copies.append(pltpu.make_async_copy(src.at[span], dst.at[span], sem.at[len(copies)]))
    for copy in copies:
        copy.start()
    for copy in copies:
        copy.wait()


def kernel(
    hidden, target, head, cot, wgrad, hgrad, div,
    tgt_in, tgt_s, head_s, part, sib_r, ya_r, yb_r, ed, et, loc, turn, stx, stz, cotcol, divcol,
    grad, hgp, xa_r, xb_r, zr, load_sem, send_sem, recv_sem, *hid_s,
):
    hid, voc = lax.axis_index("hid"), lax.axis_index("voc")
    y, core = hid // 2, hid % 2
    x, z = voc // 8, voc % 8
    vocab, depth = head.shape
    padded = part.shape[1]
    halves = (pl.ds(0, padded // 2), pl.ds(padded // 2, padded // 2))

    def at(yy=y, cc=core, xx=x, zz=z):
        return {"hid": yy * 2 + cc, "voc": xx * 8 + zz}

    yp, ym, yo = (y + 1) % 4, (y + 3) % 4, (y + 2) % 4
    xp, xm, xo = (x + 1) % 4, (x + 3) % 4, (x + 2) % 4
    sibling = at(cc=1 - core)
    partners = [sibling, at(yy=yp), at(yy=ym)]
    partners += [at(xx=(x + d) % 4) for d in (1, 2, 3)]
    partners += [at(zz=(z + d) % 8) for d in range(1, 8)]

    barrier = pltpu.get_barrier_semaphore()
    for partner in partners:
        pl.semaphore_signal(barrier, inc=1, device_id=partner, device_id_type=MESH)

    loads = {}

    def load(name, src, dst):
        copy = pltpu.make_async_copy(src, dst, load_sem.at[sum(map(len, loads.values()))])
        copy.start()
        loads.setdefault(name, []).append(copy)

    def load_hidden(c):
        for i, g in enumerate(CHUNKS[c]):
            for k in (0, 1):
                load(c, hidden.at[:, k, g], hid_s[c].at[k, :, i])

    def loaded(name):
        for copy in loads[name]:
            copy.wait()

    load_hidden(0)
    for i in range(0, vocab, 512):
        span = pl.ds(i, min(512, vocab - i))
        load("head", head.at[span], head_s.at[span])
    load("target", target.at[:, pl.ds(pl.multiple_of(hid * 128, 128), 128)], tgt_in)
    load("cot", cot, cotcol.at[pl.ds(0, 8)])
    for c in range(1, N):
        load_hidden(c)

    copies = {}

    def remote(name, src, dst, device):
        n = len(copies)
        copy = pltpu.make_async_remote_copy(
            src_ref=src, dst_ref=dst, send_sem=send_sem.at[n], recv_sem=recv_sem.at[n],
            device_id=device, device_id_type=MESH,
        )
        copies[name] = copy
        return copy

    def send(name, src, dst, device):
        remote(name, src, dst, device).start()

    def arrived(name):
        copies[name].wait_recv()

    def span(base, count):
        return pl.ds(base if isinstance(base, int) else pl.multiple_of(base, 16), count)

    def rows(c, yy, cc=core):
        return span(8 * BASE[c] + cc * 4 * SIZE[c] + yy * SIZE[c], SIZE[c])

    def chunk(c):
        return pl.ds(BASE[c], SIZE[c])

    def tiles(width):
        return [pl.ds(i, min(width, vocab - i)) for i in range(0, vocab, width)]

    def hidden_rows(c):
        return hid_s[c][...].reshape(8 * SIZE[c], depth)

    def stage_m(c):
        loaded(c)
        if c == 0:
            loaded("head")
        mine = pl.ds(8 * BASE[c], 8 * SIZE[c])
        for cols in tiles(512):
            part[mine, cols] = lax.dot_general(
                hidden_rows(c), head_s[cols, :], (((1,), (1,)), ((), ())), preferred_element_type=F32
            )
        part[mine, vocab:padded] = jnp.zeros((8 * SIZE[c], padded - vocab), F32)
        if c == 0:
            pl.semaphore_wait(barrier, len(partners))
        theirs = span(8 * BASE[c] + (1 - core) * 4 * SIZE[c], 4 * SIZE[c])
        send(f"sib{c}", part.at[theirs], sib_r.at[pl.ds(4 * BASE[c], 4 * SIZE[c])], sibling)

    def add_sibling(c, yy):
        mine = rows(c, yy)
        part[mine, :] = part[mine, :] + sib_r[span(4 * BASE[c] + yy * SIZE[c], SIZE[c]), :]

    def stage_a(c):
        low, high = halves
        arrived(f"sib{c}")
        add_sibling(c, yo)
        send(f"yap{c}", part.at[rows(c, yo), low], ya_r.at[0, chunk(c)], at(yy=yp))
        send(f"yam{c}", part.at[rows(c, yo), high], ya_r.at[1, chunk(c)], at(yy=ym))
        add_sibling(c, yp)
        send(f"ydp{c}", part.at[rows(c, yp), high], yb_r.at[0, chunk(c), high], at(yy=yp))
        add_sibling(c, ym)
        send(f"ydm{c}", part.at[rows(c, ym), low], yb_r.at[1, chunk(c), low], at(yy=ym))
        add_sibling(c, y)

    def stage_b(c):
        low, high = halves
        arrived(f"yap{c}")
        part[rows(c, yp), low] = part[rows(c, yp), low] + ya_r[0, chunk(c)]
        send(f"ybp{c}", part.at[rows(c, yp), low], yb_r.at[0, chunk(c), low], at(yy=yp))
        arrived(f"yam{c}")
        part[rows(c, ym), high] = part[rows(c, ym), high] + ya_r[1, chunk(c)]
        send(f"ybm{c}", part.at[rows(c, ym), high], yb_r.at[1, chunk(c), high], at(yy=ym))

    def own_rows(c):
        return [pl.ds(16 * g, 16) for g in CHUNKS[c]]

    def stage_t(_):
        turn[...] = jnp.zeros_like(turn)
        loaded("cot")
        cotcol[...] = jnp.broadcast_to(cotcol[pl.ds(hid, 1), :], (128, 128)).T
        loaded("target")
        tgt_s[...] = tgt_in[...].astype(F32).T

    def stage_l(c):
        for name in ("ydp", "ydm", "ybp", "ybm"):
            arrived(f"{name}{c}")
        d = part[rows(c, y), 0:vocab] + yb_r[0, chunk(c), 0:vocab] + yb_r[1, chunk(c), 0:vocab]
        t = jnp.concatenate([tgt_s[r, :] for r in own_rows(c)], axis=0)
        top_d = jnp.max(d, axis=1, keepdims=True)
        top_t = jnp.max(t, axis=1, keepdims=True)
        exp_d = jnp.exp(d - top_d)
        exp_t = jnp.exp(t - top_t)
        ed[chunk(c), :] = exp_d
        et[chunk(c), :] = exp_t
        sum_d = jnp.sum(exp_d, axis=1, keepdims=True)
        sum_t = jnp.sum(exp_t, axis=1, keepdims=True)
        numer = jnp.sum(exp_t * (t - d), axis=1, keepdims=True)
        lane = lax.broadcasted_iota(jnp.int32, (SIZE[c], 128), 1)
        both = jnp.zeros((SIZE[c], 128), F32)
        for k, column in enumerate((top_d, sum_d, top_t, sum_t, numer)):
            both = jnp.where(lane == k, column, both)
        loc[chunk(c), :] = both
        turn[pl.ds(0, SIZE[c]), :] = both
        stx[c, x] = turn[...].T[0:8, :]
        for d_ in (1, 2, 3):
            send(f"sx{d_}_{c}", stx.at[c, x], stx.at[c, x], at(xx=(x + d_) % 4))

    def merge(stats):
        top_d, top_t = stats[0][0:1], stats[0][2:3]
        for s in stats[1:]:
            top_d, top_t = jnp.maximum(top_d, s[0:1]), jnp.maximum(top_t, s[2:3])
        sum_d = sum_t = numer = jnp.zeros((1, 128), F32)
        for s in stats:
            scale_d, scale_t = jnp.exp(s[0:1] - top_d), jnp.exp(s[2:3] - top_t)
            sum_d, sum_t = sum_d + s[1:2] * scale_d, sum_t + s[3:4] * scale_t
            numer = numer + s[4:5] * scale_t
        return top_d, sum_d, top_t, sum_t, numer

    def stack(values):
        sub = lax.broadcasted_iota(jnp.int32, (8, 128), 0)
        both = jnp.zeros((8, 128), F32)
        for k, row in enumerate(values):
            both = jnp.where(sub == k, row, both)
        return both

    def stage_x(c):
        for d_ in (1, 2, 3):
            arrived(f"sx{d_}_{c}")
        stz[c, z] = stack(merge([stx[c, i] for i in range(4)]))
        for d_ in range(1, 8):
            send(f"sz{d_}_{c}", stz.at[c, z], stz.at[c, z], at(zz=(z + d_) % 8))

    def stage_g(c):
        for d_ in range(1, 8):
            arrived(f"sz{d_}_{c}")
        top_d, sum_d, top_t, sum_t, numer = merge([stz[c, i] for i in range(8)])
        norm_d, norm_t = top_d + jnp.log(sum_d), top_t + jnp.log(sum_t)
        divergence = numer / sum_t + norm_d - norm_t
        turn[pl.ds(0, 8), :] = stack((norm_d, norm_t, divergence))
        columns = turn[...].T[0 : SIZE[c], :]
        weight = jnp.concatenate([cotcol[r, :] for r in own_rows(c)], axis=0)[:, 0:1]
        for i, r in enumerate(own_rows(c)):
            divcol[r, :] = jnp.broadcast_to(columns[16 * i : 16 * i + 16, 2:3], (16, 128))
        both = loc[chunk(c), :]
        scale_d = weight * jnp.exp(both[:, 0:1] - columns[:, 0:1])
        scale_t = weight * jnp.exp(both[:, 2:3] - columns[:, 1:2])
        mine = rows(c, y)
        grad[mine, 0:vocab] = (ed[chunk(c), :] * scale_d - et[chunk(c), :] * scale_t).astype(BF16)
        grad[mine, vocab:padded] = jnp.zeros((SIZE[c], padded - vocab), BF16)
        block = grad.at[mine]
        send(f"gp{c}", block, block, at(yy=yp))
        send(f"gm{c}", block, block, at(yy=ym))
        send(f"gs{c}", block, block, sibling)

    def stage_f(c):
        low, high = halves
        arrived(f"gp{c}")
        part_of = grad.at[rows(c, ym), low]
        send(f"fp{c}", part_of, part_of, at(yy=yp))
        block = grad.at[rows(c, ym)]
        send(f"fsm{c}", block, block, sibling)
        arrived(f"gm{c}")
        part_of = grad.at[rows(c, yp), high]
        send(f"fm{c}", part_of, part_of, at(yy=ym))
        block = grad.at[rows(c, yp)]
        send(f"fsp{c}", block, block, sibling)

    def stage_h(c):
        arrived(f"fp{c}")
        arrived(f"fm{c}")
        block = grad.at[rows(c, yo)]
        send(f"hs{c}", block, block, sibling)

    def hrows(c, xx, k, count=1):
        return span(8 * BASE[c] + xx * 2 * SIZE[c] + k * SIZE[c], count * SIZE[c])

    def stage_k(c):
        for name in ("gs", "fsm", "fsp", "hs"):
            arrived(f"{name}{c}")
        out = jnp.dot(
            grad[pl.ds(8 * BASE[c], 8 * SIZE[c]), 0:vocab], head_s[...], preferred_element_type=F32
        )
        for k in (0, 1):
            for xx in range(4):
                start = (k * 4 + xx) * SIZE[c]
                hgp[hrows(c, xx, k), :] = out[start : start + SIZE[c]]
        both = (pl.ds(2 * BASE[c], SIZE[c]), pl.ds(2 * BASE[c] + SIZE[c], SIZE[c]))
        send(f"xap{c}", hgp.at[hrows(c, xo, 0)], xa_r.at[0, chunk(c)], at(xx=xp))
        send(f"xam{c}", hgp.at[hrows(c, xo, 1)], xa_r.at[1, chunk(c)], at(xx=xm))
        send(f"xdp{c}", hgp.at[hrows(c, xp, 1)], xb_r.at[0, both[1]], at(xx=xp))
        send(f"xdm{c}", hgp.at[hrows(c, xm, 0)], xb_r.at[1, both[0]], at(xx=xm))

    def stage_r(c):
        both = (pl.ds(2 * BASE[c], SIZE[c]), pl.ds(2 * BASE[c] + SIZE[c], SIZE[c]))
        arrived(f"xap{c}")
        mine = hrows(c, xp, 0)
        hgp[mine, :] = hgp[mine, :] + xa_r[0, chunk(c)]
        send(f"xbp{c}", hgp.at[mine], xb_r.at[0, both[0]], at(xx=xp))
        arrived(f"xam{c}")
        mine = hrows(c, xm, 1)
        hgp[mine, :] = hgp[mine, :] + xa_r[1, chunk(c)]
        send(f"xbm{c}", hgp.at[mine], xb_r.at[1, both[1]], at(xx=xm))

    def zrows(c, k, i):
        return span(8 * BASE[c] + x * 2 * SIZE[c] + k * SIZE[c] + i * 16, 16)

    def stage_z(c):
        for name in ("xdp", "xdm", "xbp", "xbm"):
            arrived(f"{name}{c}")
        mine = hrows(c, x, 0, 2)
        both = pl.ds(2 * BASE[c], 2 * SIZE[c])
        hgp[mine, :] = hgp[mine, :] + xb_r[0, both] + xb_r[1, both]
        for d_ in range(1, 8):
            zz = (z + d_) % 8
            for i, g in enumerate(CHUNKS[c]):
                copy = remote(f"z{d_}{i}{c}", hgp.at[zrows(c, zz // 4, i)], zr.at[c, d_ - 1], at(zz=zz))
                pl.when(zz % 4 == g // 2)(copy.start)

    def stage_o(c):
        for i, g in enumerate(CHUNKS[c]):

            @pl.when(z % 4 == g // 2)
            def _():
                total = hgp[zrows(c, z // 4, i), :]
                for d_ in range(1, 8):
                    arrived(f"z{d_}{i}{c}")
                    total = total + zr[c, d_ - 1]
                hgrad[pl.ds(16 * (g % 2), 16), :] = total.astype(BF16)

    def stage_w(quarter):
        for cols in tiles(WIDE)[2 * quarter : 2 * quarter + 2]:
            total = None
            for c in range(N):
                term = lax.dot_general(
                    grad[pl.ds(8 * BASE[c], 8 * SIZE[c]), cols], hidden_rows(c),
                    (((0,), (0,)), ((), ())), preferred_element_type=F32,
                )
                total = term if total is None else total + term
            wgrad[cols, :] = total.astype(BF16)

    stages = {
        "M": stage_m, "A": stage_a, "B": stage_b, "L": stage_l, "X": stage_x, "G": stage_g, "F": stage_f,
        "H": stage_h, "K": stage_k, "R": stage_r, "Z": stage_z, "O": stage_o, "W": stage_w, "T": stage_t,
    }
    for entry in ORDER:
        stages[entry[0]](int(entry[1]))

    div[...] = divcol[...].T[0:1, :]
    for name, copy in copies.items():
        if name[0] == "z":
            d_, i, c = (int(v) for v in name[1:])
            pl.when((z + d_) % 4 == CHUNKS[c][i] // 2)(copy.wait_send)
        else:
            copy.wait_send()


def per_device(hidden, target, head, cotangent):
    depth, vocab = head.shape
    padded = -(-vocab // 256) * 256
    vmem = pltpu.VMEM
    results = (
        jax.ShapeDtypeStruct((vocab, depth), BF16),
        jax.ShapeDtypeStruct((32, depth), BF16),
        jax.ShapeDtypeStruct((1, 128), F32),
    )
    wgrad, hgrad, div = pl.pallas_call(
        kernel,
        out_shape=tuple(vmem(r.shape, r.dtype) for r in results),
        in_specs=[pl.BlockSpec(memory_space=pltpu.HBM)] * 4,
        out_specs=(pl.BlockSpec(memory_space=vmem),) * 3,
        scratch_shapes=[
            vmem((vocab, 128), BF16),
            vmem((128, vocab), F32),
            vmem((vocab, depth), BF16),
            vmem((1024, padded), F32),
            vmem((512, padded), F32),
            vmem((2, 128, padded // 2), F32),
            vmem((2, 128, padded), F32),
            vmem((128, vocab), F32),
            vmem((128, vocab), F32),
            vmem((128, 128), F32),
            vmem((128, 128), F32),
            vmem((N, 4, 8, 128), F32),
            vmem((N, 8, 8, 128), F32),
            vmem((128, 128), F32),
            vmem((128, 128), F32),
            vmem((1024, padded), BF16),
            vmem((1024, depth), F32),
            vmem((2, 128, depth), F32),
            vmem((2, 256, depth), F32),
            vmem((N, 7, 16, depth), F32),
            pltpu.SemaphoreType.DMA((48,)),
            pltpu.SemaphoreType.DMA((46 * N,)),
            pltpu.SemaphoreType.DMA((46 * N,)),
        ]
        + [vmem((2, 4, len(groups), 16, depth), BF16) for groups in CHUNKS],
        compiler_params=pltpu.CompilerParams(
            collective_id=0, has_side_effects=True, vmem_limit_bytes=52 * 1024 * 1024
        ),
    )(
        *(
            pltpu.with_memory_space_constraint(v, pltpu.HBM)
            for v in (hidden.reshape(4, 2, 8, 16, depth), target.T, head.T, cotangent.reshape(8, 128))
        )
    )
    wgrad, hgrad, div = pl.pallas_call(
        place,
        out_shape=results,
        in_specs=[pl.BlockSpec(memory_space=vmem)] * 3,
        out_specs=(pl.BlockSpec(memory_space=pltpu.HBM),) * 3,
        scratch_shapes=[pltpu.SemaphoreType.DMA((16,))],
        compiler_params=pltpu.CompilerParams(vmem_limit_bytes=1024 * 1024),
    )(*(pltpu.with_memory_space_constraint(v, vmem) for v in (wgrad, hgrad, div)))
    return hgrad, wgrad.T, div.reshape(128)


def solution(mesh):
    return jax.shard_map(
        per_device,
        mesh=mesh,
        in_specs=(P(None, "hid"), P(None, "voc"), P("hid", "voc"), P()),
        out_specs=(P("voc", "hid"), P("hid", "voc"), P("hid")),
        check_vma=False,
    )
```

time: 588 us -> 102 us (0.17)
  waiting for transfers between devices: 350 us -> 0 us
  blocking collectives: 172 us -> 0 us
  Pallas kernels: 0 us -> 101 us
  matrix products: 23.3 us -> 0 us
  other arithmetic: 20.6 us -> 0 us
  between operations: 14.1 us -> 0.8 us
    reduce_scatter x1 -> x0, waiting for transfers between devices: 241 us -> none  [per_device(): lax.psum_scatter(lax.dot_general(grad_all, head, (((1,), (1,)), ((), ()))...]
    psum x1 -> x0, blocking collectives: 110 us -> none  [softmax_grad(): lax.psum((jnp.sum(exp_d, axis=-1), jnp.sum(exp_t, axis=-1), jnp.sum(exp_t...]
    psum x1 -> x0, waiting for transfers between devices: 109 us -> none  [per_device(): draft = lax.psum(partial_logits, 'hid')]
    pallas_call x0 -> x2, Pallas kernels: none -> 101 us  [the longest x1 99.4 us: per_device(): pl.pallas_call(kernel, out_shape=tuple((vmem(r.shape, r.dtype) for r in r...]
    pmax x1 -> x0, blocking collectives: 62.1 us -> none  [softmax_grad(): peak_d, peak_t = lax.pmax((peak_d, peak_t), 'voc')]
    dot_general x3 -> x0, matrix products: 23.3 us -> none  [the longest x1 8.75 us: per_device(): partial_logits = jnp.dot(hidden, head, preferred_element_type=jnp.float32)]
    convert_element_type x2 -> x0, other arithmetic: 7.57 us -> none  [the longest x1 6.04 us: softmax_grad(): grad = (cotangent[:, None] * (probs_q - probs_p)).astype(jnp.bfloat16)]
    reduce_max x2 -> x0, other arithmetic: 6.74 us -> none  [the longest x1 3.87 us: softmax_grad(): peak_d = jnp.max(draft, axis=-1)]
  transfers between devices with their start and end apart: 2 -> 0, of which waited for: 2 -> 0; matrix products, arithmetic and copies ran while one was open for 2% -> 0% of each run, Pallas kernels for 0% -> 0%
where the time goes in v1:
time: 102 us
  Pallas kernels  101 us (99%)
    pallas_call x1, Pallas kernels, per_device(): pl.pallas_call(kernel, out_shape=tuple((vmem(r.shape, r.dtype) for r in r...  99.4 us

profile of v1, /device:TPU:1, one launch (start us, length us, event | category | flops | bytes accessed | tf_op | source)
XLA Modules:
  0.0 102.2 jit_solution(1409738760808563344)
XLA Ops:
  0.6 99.4 %shard_map.67 = (bf16[2020,896]{1,0:T(8,128)(2,1)S(1)}, bf16[32,896]{1,0:T(8,128)(2,1)S(1)}, f32[1,128]{1,0:T(1,128)S(1)}) custom-call(bf16[4,2,8,16,896]{4,3,2,1,0:T(8,128)(2,1)} %bitcast.8, bf16[2020,1024]{1,0:T(8,128)(2,1)} %bitcast.6, bf16[2020,896]{1,0:T(8,128)(2,1)} %bitcast.7, f32[8,128]{1,0:T(8,128)} %bitcast.9), custom_call_target="tpu_custom_call" | custom-call | tf_op jit(solution)/shard_map/pallas_call | solution.py:352
  100.0 2.0 %shard_map.68 = (bf16[2020,896]{1,0:T(8,128)(2,1)}, bf16[32,896]{1,0:T(8,128)(2,1)}, f32[1,128]{1,0:T(1,128)}) custom-call(bf16[2020,896]{1,0:T(8,128)(2,1)S(1)} %get-tuple-element.9.refs_0_, bf16[32,896]{1,0:T(8,128)(2,1)S(1)} %get-tuple-element.10.refs_1_, f32[1,128]{1,0:T(1,128)S(1)} %get-tuple-element.11.refs_2_), custom_call_target="tpu_custom_call" | custom-call | tf_op jit(solution)/shard_map/pallas_call | solution.py:392

commit v2 on v1

--- a/solution.py
+++ b/solution.py
@@ -12,12 +12,41 @@
 SIZE = [16 * len(groups) for groups in CHUNKS]
 BASE = [sum(SIZE[:c]) for c in range(N)]
 WIDE = 256
+EARLY = 3
 ORDER = (
-    "M0", "M1", "A0", "A1", "T0", "M2", "B0", "B1", "A2", "L0", "X0", "M3", "L1", "B2", "G0", "M4", "X1", "A3",
-    "L2", "F0", "X2", "G1", "H0", "B3", "K0", "F1", "G2", "L3", "R0", "H1", "A4", "K1", "X3", "F2", "Z0", "B4",
-    "G3", "H2", "R1", "L4", "K2", "X4", "F3", "Z1", "R2", "H3", "G4", "K3", "F4", "Z2", "R3", "H4", "O1", "K4",
-    "Z3", "O0", "R4", "O2", "Z4", "W2", "W1", "W3", "O3", "W0", "O4",
+    "M0", "M1", "A0", "A1", "T0", "B0", "M2", "B1", "A2", "L0", "M3", "X0", "L1", "B2", "M4", "G0", "A3", "X1",
+    "L2", "F0", "G1", "X2", "H0", "B3", "K0", "F1", "G2", "L3", "R0", "H1", "A4", "X3", "K1", "F2", "B4", "G3",
+    "R1", "Z0", "H2", "L4", "K2", "X4", "F3", "Z1", "V2", "V0", "H3", "R2", "G4", "K3", "Z2", "F4", "R3", "V1",
+    "H4", "K4", "Z3", "R4", "W1", "Z4", "O2", "W2", "O1", "V3", "W0", "W3", "O3", "O0", "O4",
 )
+
+
+def pack(value):
+    width = value.shape[1]
+    half = -(-width // 256) * 128
+    top = value.astype(BF16)
+    near = top.astype(F32)
+    rest = (value - near) * (256.0 * 127.0) * pltpu.reciprocal(jnp.maximum(jnp.abs(near), 1e-30), approx=True)
+    first, second = rest[:, :half], rest[:, half:] * (63.0 / 127.0)
+    if width < 2 * half:
+        second = jnp.concatenate([second, jnp.zeros((value.shape[0], 2 * half - width), F32)], axis=1)
+    first = jnp.round(jnp.clip(first, -127.0, 127.0))
+    second = jnp.round(jnp.clip(second, -63.0, 63.0))
+    size = 128.0 + jnp.abs(first)
+    word = jnp.where(first < 0, -size, size) * jnp.exp2(second)
+    return jnp.concatenate([top, word.astype(BF16)], axis=1)
+
+
+def unpack(packed, width):
+    half = -(-width // 256) * 128
+    near = packed[:, :width].astype(F32)
+    word = packed[:, width:].astype(F32)
+    size = jnp.abs(word)
+    second = jnp.floor(jnp.log2(size) + 0.001) - 7.0
+    first = jnp.round(size * jnp.exp2(-second)) - 128.0
+    first = jnp.where(word < 0, -first, first)
+    rest = jnp.concatenate([first * (1 / 127.0), second[:, : width - half] * (1 / 63.0)], axis=1)
+    return near + rest * jnp.abs(near) * (1 / 256.0)
 
 
 def place(*refs):
@@ -36,8 +65,8 @@
 
 def kernel(
     hidden, target, head, cot, wgrad, hgrad, div,
-    tgt_in, tgt_s, head_s, part, sib_r, ya_r, yb_r, ed, et, loc, turn, stx, stz, cotcol, divcol,
-    grad, hgp, xa_r, xb_r, zr, load_sem, send_sem, recv_sem, *hid_s,
+    tgt_in, tgt_s, head_s, part, sib_r, ys, ya_r, yb_r, ed, et, loc, turn, stx, stz, cotcol, divcol,
+    early, grad, hgp, xs, xa_r, xb_r, zs, zr, load_sem, send_sem, recv_sem, *hid_s,
 ):
     hid, voc = lax.axis_index("hid"), lax.axis_index("voc")
     y, core = hid // 2, hid % 2
@@ -132,30 +161,29 @@
         theirs = span(8 * BASE[c] + (1 - core) * 4 * SIZE[c], 4 * SIZE[c])
         send(f"sib{c}", part.at[theirs], sib_r.at[pl.ds(4 * BASE[c], 4 * SIZE[c])], sibling)
 
-    def add_sibling(c, yy):
-        mine = rows(c, yy)
-        part[mine, :] = part[mine, :] + sib_r[span(4 * BASE[c] + yy * SIZE[c], SIZE[c]), :]
+    def partial(c, yy, half):
+        return part[rows(c, yy), half] + sib_r[span(4 * BASE[c] + yy * SIZE[c], SIZE[c]), half]
+
+    def send_packed(name, c, buffer, value, dst, device):
+        buffer[chunk(c), :] = pack(value)
+        send(f"{name}{c}", buffer.at[chunk(c)], dst, device)
 
     def stage_a(c):
         low, high = halves
         arrived(f"sib{c}")
-        add_sibling(c, yo)
-        send(f"yap{c}", part.at[rows(c, yo), low], ya_r.at[0, chunk(c)], at(yy=yp))
-        send(f"yam{c}", part.at[rows(c, yo), high], ya_r.at[1, chunk(c)], at(yy=ym))
-        add_sibling(c, yp)
-        send(f"ydp{c}", part.at[rows(c, yp), high], yb_r.at[0, chunk(c), high], at(yy=yp))
-        add_sibling(c, ym)
-        send(f"ydm{c}", part.at[rows(c, ym), low], yb_r.at[1, chunk(c), low], at(yy=ym))
-        add_sibling(c, y)
+        send_packed("yap", c, ys.at[0], partial(c, yo, low), ya_r.at[0, chunk(c)], at(yy=yp))
+        send_packed("yam", c, ys.at[1], partial(c, yo, high), ya_r.at[1, chunk(c)], at(yy=ym))
+        send_packed("ydp", c, ys.at[2], partial(c, yp, high), yb_r.at[0, 1, chunk(c)], at(yy=yp))
+        send_packed("ydm", c, ys.at[3], partial(c, ym, low), yb_r.at[1, 0, chunk(c)], at(yy=ym))
 
     def stage_b(c):
         low, high = halves
         arrived(f"yap{c}")
-        part[rows(c, yp), low] = part[rows(c, yp), low] + ya_r[0, chunk(c)]
-        send(f"ybp{c}", part.at[rows(c, yp), low], yb_r.at[0, chunk(c), low], at(yy=yp))
+        total = partial(c, yp, low) + unpack(ya_r[0, chunk(c)], padded // 2)
+        send_packed("ybp", c, ys.at[4], total, yb_r.at[0, 0, chunk(c)], at(yy=yp))
         arrived(f"yam{c}")
-        part[rows(c, ym), high] = part[rows(c, ym), high] + ya_r[1, chunk(c)]
-        send(f"ybm{c}", part.at[rows(c, ym), high], yb_r.at[1, chunk(c), high], at(yy=ym))
+        total = partial(c, ym, high) + unpack(ya_r[1, chunk(c)], padded // 2)
+        send_packed("ybm", c, ys.at[5], total, yb_r.at[1, 1, chunk(c)], at(yy=ym))
 
     def own_rows(c):
         return [pl.ds(16 * g, 16) for g in CHUNKS[c]]
@@ -170,7 +198,13 @@
     def stage_l(c):
         for name in ("ydp", "ydm", "ybp", "ybm"):
             arrived(f"{name}{c}")
-        d = part[rows(c, y), 0:vocab] + yb_r[0, chunk(c), 0:vocab] + yb_r[1, chunk(c), 0:vocab]
+        d = [
+            partial(c, y, half)
+            + unpack(yb_r[0, i, chunk(c)], padded // 2)
+            + unpack(yb_r[1, i, chunk(c)], padded // 2)
+            for i, half in enumerate(halves)
+        ]
+        d = jnp.concatenate([d[0], d[1][:, : vocab - padded // 2]], axis=1)
         t = jnp.concatenate([tgt_s[r, :] for r in own_rows(c)], axis=0)
         top_d = jnp.max(d, axis=1, keepdims=True)
         top_t = jnp.max(t, axis=1, keepdims=True)
@@ -270,22 +304,18 @@
             for xx in range(4):
                 start = (k * 4 + xx) * SIZE[c]
                 hgp[hrows(c, xx, k), :] = out[start : start + SIZE[c]]
-        both = (pl.ds(2 * BASE[c], SIZE[c]), pl.ds(2 * BASE[c] + SIZE[c], SIZE[c]))
-        send(f"xap{c}", hgp.at[hrows(c, xo, 0)], xa_r.at[0, chunk(c)], at(xx=xp))
-        send(f"xam{c}", hgp.at[hrows(c, xo, 1)], xa_r.at[1, chunk(c)], at(xx=xm))
-        send(f"xdp{c}", hgp.at[hrows(c, xp, 1)], xb_r.at[0, both[1]], at(xx=xp))
-        send(f"xdm{c}", hgp.at[hrows(c, xm, 0)], xb_r.at[1, both[0]], at(xx=xm))
+        send_packed("xap", c, xs.at[0], hgp[hrows(c, xo, 0), :], xa_r.at[0, chunk(c)], at(xx=xp))
+        send_packed("xam", c, xs.at[1], hgp[hrows(c, xo, 1), :], xa_r.at[1, chunk(c)], at(xx=xm))
+        send_packed("xdp", c, xs.at[2], hgp[hrows(c, xp, 1), :], xb_r.at[0, 1, chunk(c)], at(xx=xp))
+        send_packed("xdm", c, xs.at[3], hgp[hrows(c, xm, 0), :], xb_r.at[1, 0, chunk(c)], at(xx=xm))
 
     def stage_r(c):
-        both = (pl.ds(2 * BASE[c], SIZE[c]), pl.ds(2 * BASE[c] + SIZE[c], SIZE[c]))
         arrived(f"xap{c}")
-        mine = hrows(c, xp, 0)
-        hgp[mine, :] = hgp[mine, :] + xa_r[0, chunk(c)]
-        send(f"xbp{c}", hgp.at[mine], xb_r.at[0, both[0]], at(xx=xp))
+        total = hgp[hrows(c, xp, 0), :] + unpack(xa_r[0, chunk(c)], depth)
+        send_packed("xbp", c, xs.at[4], total, xb_r.at[0, 0, chunk(c)], at(xx=xp))
         arrived(f"xam{c}")
-        mine = hrows(c, xm, 1)
-        hgp[mine, :] = hgp[mine, :] + xa_r[1, chunk(c)]
-        send(f"xbm{c}", hgp.at[mine], xb_r.at[1, both[1]], at(xx=xm))
+        total = hgp[hrows(c, xm, 1), :] + unpack(xa_r[1, chunk(c)], depth)
+        send_packed("xbm", c, xs.at[5], total, xb_r.at[1, 1, chunk(c)], at(xx=xm))
 
     def zrows(c, k, i):
         return span(8 * BASE[c] + x * 2 * SIZE[c] + k * SIZE[c] + i * 16, 16)
@@ -293,13 +323,16 @@
     def stage_z(c):
         for name in ("xdp", "xdm", "xbp", "xbm"):
             arrived(f"{name}{c}")
-        mine = hrows(c, x, 0, 2)
-        both = pl.ds(2 * BASE[c], 2 * SIZE[c])
-        hgp[mine, :] = hgp[mine, :] + xb_r[0, both] + xb_r[1, both]
+        for k in (0, 1):
+            total = hgp[hrows(c, x, k), :]
+            total = total + unpack(xb_r[0, k, chunk(c)], depth) + unpack(xb_r[1, k, chunk(c)], depth)
+            hgp[hrows(c, x, k), :] = total
+            zs[k, chunk(c), :] = pack(total)
         for d_ in range(1, 8):
             zz = (z + d_) % 8
             for i, g in enumerate(CHUNKS[c]):
-                copy = remote(f"z{d_}{i}{c}", hgp.at[zrows(c, zz // 4, i)], zr.at[c, d_ - 1], at(zz=zz))
+                block = zs.at[zz // 4, pl.ds(BASE[c] + 16 * i, 16)]
+                copy = remote(f"z{d_}{i}{c}", block, zr.at[c, d_ - 1], at(zz=zz))
                 pl.when(zz % 4 == g // 2)(copy.start)
 
     def stage_o(c):
@@ -310,23 +343,30 @@
                 total = hgp[zrows(c, z // 4, i), :]
                 for d_ in range(1, 8):
                     arrived(f"z{d_}{i}{c}")
-                    total = total + zr[c, d_ - 1]
+                    total = total + unpack(zr[c, d_ - 1], depth)
                 hgrad[pl.ds(16 * (g % 2), 16), :] = total.astype(BF16)
+
+    def head_term(cols, chunks):
+        total = None
+        for c in chunks:
+            term = lax.dot_general(
+                grad[pl.ds(8 * BASE[c], 8 * SIZE[c]), cols], hidden_rows(c),
+                (((0,), (0,)), ((), ())), preferred_element_type=F32,
+            )
+            total = term if total is None else total + term
+        return total
+
+    def stage_v(quarter):
+        for cols in tiles(WIDE)[2 * quarter : 2 * quarter + 2]:
+            early[cols, :] = head_term(cols, range(EARLY))
 
     def stage_w(quarter):
         for cols in tiles(WIDE)[2 * quarter : 2 * quarter + 2]:
-            total = None
-            for c in range(N):
-                term = lax.dot_general(
-                    grad[pl.ds(8 * BASE[c], 8 * SIZE[c]), cols], hidden_rows(c),
-                    (((0,), (0,)), ((), ())), preferred_element_type=F32,
-                )
-                total = term if total is None else total + term
-            wgrad[cols, :] = total.astype(BF16)
+            wgrad[cols, :] = (early[cols, :] + head_term(cols, range(EARLY, N))).astype(BF16)
 
     stages = {
         "M": stage_m, "A": stage_a, "B": stage_b, "L": stage_l, "X": stage_x, "G": stage_g, "F": stage_f,
-        "H": stage_h, "K": stage_k, "R": stage_r, "Z": stage_z, "O": stage_o, "W": stage_w, "T": stage_t,
+        "H": stage_h, "K": stage_k, "R": stage_r, "Z": stage_z, "O": stage_o, "V": stage_v, "W": stage_w, "T": stage_t,
     }
     for entry in ORDER:
         stages[entry[0]](int(entry[1]))
@@ -343,6 +383,7 @@
 def per_device(hidden, target, head, cotangent):
     depth, vocab = head.shape
     padded = -(-vocab // 256) * 256
+    wide = depth + -(-depth // 256) * 128
     vmem = pltpu.VMEM
     results = (
         jax.ShapeDtypeStruct((vocab, depth), BF16),
@@ -360,8 +401,9 @@
             vmem((vocab, depth), BF16),
             vmem((1024, padded), F32),
             vmem((512, padded), F32),
-            vmem((2, 128, padded // 2), F32),
-            vmem((2, 128, padded), F32),
+            vmem((6, 128, padded * 3 // 4), BF16),
+            vmem((2, 128, padded * 3 // 4), BF16),
+            vmem((2, 2, 128, padded * 3 // 4), BF16),
             vmem((128, vocab), F32),
             vmem((128, vocab), F32),
             vmem((128, 128), F32),
@@ -370,18 +412,21 @@
             vmem((N, 8, 8, 128), F32),
             vmem((128, 128), F32),
             vmem((128, 128), F32),
+            vmem((vocab, depth), F32),
             vmem((1024, padded), BF16),
             vmem((1024, depth), F32),
-            vmem((2, 128, depth), F32),
-            vmem((2, 256, depth), F32),
-            vmem((N, 7, 16, depth), F32),
+            vmem((6, 128, wide), BF16),
+            vmem((2, 128, wide), BF16),
+            vmem((2, 2, 128, wide), BF16),
+            vmem((2, 128, wide), BF16),
+            vmem((N, 7, 16, wide), BF16),
             pltpu.SemaphoreType.DMA((48,)),
             pltpu.SemaphoreType.DMA((46 * N,)),
             pltpu.SemaphoreType.DMA((46 * N,)),
         ]
         + [vmem((2, 4, len(groups), 16, depth), BF16) for groups in CHUNKS],
         compiler_params=pltpu.CompilerParams(
-            collective_id=0, has_side_effects=True, vmem_limit_bytes=52 * 1024 * 1024
+            collective_id=0, has_side_effects=True, vmem_limit_bytes=54 * 1024 * 1024
         ),
     )(
         *(

time: 102 us -> 93.1 us (0.913)
  Pallas kernels: 101 us -> 92.2 us
    pallas_call x1, Pallas kernels: 99.4 us -> 90.2 us  [per_device(): pl.pallas_call(kernel, out_shape=tuple((vmem(r.shape, r.dtype) for r in r...]
where the time goes in v2:
time: 93.1 us; the launch traced here: 93 us
  Pallas kernels  92.2 us (99%)
    pallas_call x1, Pallas kernels, per_device(): pl.pallas_call(kernel, out_shape=tuple((vmem(r.shape, r.dtype) for r in r...  90.2 us
    pallas_call x1, Pallas kernels, per_device(): pl.pallas_call(place, out_shape=results, in_specs=[pl.BlockSpec(memory_sp...  1.96 us

profile of v2, /device:TPU:1, one launch (start us, length us, event | category | flops | bytes accessed | tf_op | source)
XLA Modules:
  0.0 93.0 jit_solution(13392752266421972002)
XLA Ops:
  0.6 90.2 %shard_map.67 = (bf16[2020,896]{1,0:T(8,128)(2,1)S(1)}, bf16[32,896]{1,0:T(8,128)(2,1)S(1)}, f32[1,128]{1,0:T(1,128)S(1)}) custom-call(bf16[4,2,8,16,896]{4,3,2,1,0:T(8,128)(2,1)} %bitcast.8, bf16[2020,1024]{1,0:T(8,128)(2,1)} %bitcast.6, bf16[2020,896]{1,0:T(8,128)(2,1)} %bitcast.7, f32[8,128]{1,0:T(8,128)} %bitcast.9), custom_call_target="tpu_custom_call" | custom-call | tf_op jit(solution)/shard_map/pallas_call | solution.py:393
  90.9 2.0 %shard_map.68 = (bf16[2020,896]{1,0:T(8,128)(2,1)}, bf16[32,896]{1,0:T(8,128)(2,1)}, f32[1,128]{1,0:T(1,128)}) custom-call(bf16[2020,896]{1,0:T(8,128)(2,1)S(1)} %get-tuple-element.9.refs_0_, bf16[32,896]{1,0:T(8,128)(2,1)S(1)} %get-tuple-element.10.refs_1_, f32[1,128]{1,0:T(1,128)S(1)} %get-tuple-element.11.refs_2_), custom_call_target="tpu_custom_call" | custom-call | tf_op jit(solution)/shard_map/pallas_call | solution.py:437

commit v3 on v2

--- a/solution.py
+++ b/solution.py
@@ -7,29 +7,27 @@
 
 MESH = pl.DeviceIdType.MESH
 F32, BF16 = jnp.float32, jnp.bfloat16
-CHUNKS = ((0,), (2, 4), (6, 1), (3, 5), (7,))
+CHUNKS = ((0,), (4,), (2, 6), (1, 5), (3,), (7,))
 N = len(CHUNKS)
 SIZE = [16 * len(groups) for groups in CHUNKS]
 BASE = [sum(SIZE[:c]) for c in range(N)]
 WIDE = 256
-EARLY = 3
+EARLY = 4
 ORDER = (
-    "M0", "M1", "A0", "A1", "T0", "B0", "M2", "B1", "A2", "L0", "M3", "X0", "L1", "B2", "M4", "G0", "A3", "X1",
-    "L2", "F0", "G1", "X2", "H0", "B3", "K0", "F1", "G2", "L3", "R0", "H1", "A4", "X3", "K1", "F2", "B4", "G3",
-    "R1", "Z0", "H2", "L4", "K2", "X4", "F3", "Z1", "V2", "V0", "H3", "R2", "G4", "K3", "Z2", "F4", "R3", "V1",
-    "H4", "K4", "Z3", "R4", "W1", "Z4", "O2", "W2", "O1", "V3", "W0", "W3", "O3", "O0", "O4",
+    "M0", "M1", "A0", "M2", "A1", "M3", "B0", "A2", "M4", "T0", "B1", "A3", "B2", "M5", "L0", "L1", "A5", "X0",
+    "X1", "G0", "B5", "L2", "G1", "B3", "X2", "L5", "F0", "A4", "F1", "X5", "L3", "H0", "G2", "X3", "B4", "K0",
+    "H1", "G5", "K1", "R0", "F2", "G3", "L4", "X4", "H2", "R1", "F5", "K2", "F3", "Z0", "H5", "G4", "Z1", "K5",
+    "H3", "R2", "K3", "F4", "V2", "Z2", "R5", "H4", "R3", "K4", "Z5", "Z3", "O1", "R4", "V0", "O2", "W2", "Z4",
+    "O5", "V3", "V1", "W0", "O0", "W1", "W3", "O3", "O4",
 )
 
 
 def pack(value):
-    width = value.shape[1]
-    half = -(-width // 256) * 128
+    half = value.shape[1] // 2
     top = value.astype(BF16)
     near = top.astype(F32)
     rest = (value - near) * (256.0 * 127.0) * pltpu.reciprocal(jnp.maximum(jnp.abs(near), 1e-30), approx=True)
     first, second = rest[:, :half], rest[:, half:] * (63.0 / 127.0)
-    if width < 2 * half:
-        second = jnp.concatenate([second, jnp.zeros((value.shape[0], 2 * half - width), F32)], axis=1)
     first = jnp.round(jnp.clip(first, -127.0, 127.0))
     second = jnp.round(jnp.clip(second, -63.0, 63.0))
     size = 128.0 + jnp.abs(first)
@@ -37,15 +35,15 @@
     return jnp.concatenate([top, word.astype(BF16)], axis=1)
 
 
-def unpack(packed, width):
-    half = -(-width // 256) * 128
+def unpack(packed):
+    width = packed.shape[1] * 2 // 3
     near = packed[:, :width].astype(F32)
     word = packed[:, width:].astype(F32)
     size = jnp.abs(word)
     second = jnp.floor(jnp.log2(size) + 0.001) - 7.0
     first = jnp.round(size * jnp.exp2(-second)) - 128.0
     first = jnp.where(word < 0, -first, first)
-    rest = jnp.concatenate([first * (1 / 127.0), second[:, : width - half] * (1 / 63.0)], axis=1)
+    rest = jnp.concatenate([first * (1 / 127.0), second * (1 / 63.0)], axis=1)
     return near + rest * jnp.abs(near) * (1 / 256.0)
 
 
@@ -107,12 +105,15 @@
 
     load_hidden(0)
     for i in range(0, vocab, 512):
-        span = pl.ds(i, min(512, vocab - i))
-        load("head", head.at[span], head_s.at[span])
-    load("target", target.at[:, pl.ds(pl.multiple_of(hid * 128, 128), 128)], tgt_in)
-    load("cot", cot, cotcol.at[pl.ds(0, 8)])
-    for c in range(1, N):
-        load_hidden(c)
+        rows_of = pl.ds(i, min(512, vocab - i))
+        load(f"head{i}", head.at[rows_of], head_s.at[rows_of])
+    load_hidden(1)
+
+    def load_rest():
+        load("target", target.at[:, pl.ds(pl.multiple_of(hid * 128, 128), 128)], tgt_in)
+        load("cot", cot, cotcol.at[pl.ds(0, 8)])
+        for c in range(2, N):
+            load_hidden(c)
 
     copies = {}
 
@@ -148,15 +149,16 @@
 
     def stage_m(c):
         loaded(c)
-        if c == 0:
-            loaded("head")
         mine = pl.ds(8 * BASE[c], 8 * SIZE[c])
         for cols in tiles(512):
+            if c == 0:
+                loaded(f"head{cols.start}")
             part[mine, cols] = lax.dot_general(
                 hidden_rows(c), head_s[cols, :], (((1,), (1,)), ((), ())), preferred_element_type=F32
             )
         part[mine, vocab:padded] = jnp.zeros((8 * SIZE[c], padded - vocab), F32)
         if c == 0:
+            load_rest()
             pl.semaphore_wait(barrier, len(partners))
         theirs = span(8 * BASE[c] + (1 - core) * 4 * SIZE[c], 4 * SIZE[c])
         send(f"sib{c}", part.at[theirs], sib_r.at[pl.ds(4 * BASE[c], 4 * SIZE[c])], sibling)
@@ -166,6 +168,10 @@
 
     def send_packed(name, c, buffer, value, dst, device):
         buffer[chunk(c), :] = pack(value)
+        send(f"{name}{c}", buffer.at[chunk(c)], dst, device)
+
+    def send_rounded(name, c, buffer, value, dst, device):
+        buffer[chunk(c), :] = value.astype(BF16)
         send(f"{name}{c}", buffer.at[chunk(c)], dst, device)
 
     def stage_a(c):
@@ -179,10 +185,10 @@
     def stage_b(c):
         low, high = halves
         arrived(f"yap{c}")
-        total = partial(c, yp, low) + unpack(ya_r[0, chunk(c)], padded // 2)
+        total = partial(c, yp, low) + unpack(ya_r[0, chunk(c)])
         send_packed("ybp", c, ys.at[4], total, yb_r.at[0, 0, chunk(c)], at(yy=yp))
         arrived(f"yam{c}")
-        total = partial(c, ym, high) + unpack(ya_r[1, chunk(c)], padded // 2)
+        total = partial(c, ym, high) + unpack(ya_r[1, chunk(c)])
         send_packed("ybm", c, ys.at[5], total, yb_r.at[1, 1, chunk(c)], at(yy=ym))
 
     def own_rows(c):
@@ -200,8 +206,8 @@
             arrived(f"{name}{c}")
         d = [
             partial(c, y, half)
-            + unpack(yb_r[0, i, chunk(c)], padded // 2)
-            + unpack(yb_r[1, i, chunk(c)], padded // 2)
+            + unpack(yb_r[0, i, chunk(c)])
+            + unpack(yb_r[1, i, chunk(c)])
             for i, half in enumerate(halves)
         ]
         d = jnp.concatenate([d[0], d[1][:, : vocab - padded // 2]], axis=1)
@@ -304,18 +310,18 @@
             for xx in range(4):
                 start = (k * 4 + xx) * SIZE[c]
                 hgp[hrows(c, xx, k), :] = out[start : start + SIZE[c]]
-        send_packed("xap", c, xs.at[0], hgp[hrows(c, xo, 0), :], xa_r.at[0, chunk(c)], at(xx=xp))
-        send_packed("xam", c, xs.at[1], hgp[hrows(c, xo, 1), :], xa_r.at[1, chunk(c)], at(xx=xm))
-        send_packed("xdp", c, xs.at[2], hgp[hrows(c, xp, 1), :], xb_r.at[0, 1, chunk(c)], at(xx=xp))
-        send_packed("xdm", c, xs.at[3], hgp[hrows(c, xm, 0), :], xb_r.at[1, 0, chunk(c)], at(xx=xm))
+        send_rounded("xap", c, xs.at[0], hgp[hrows(c, xo, 0), :], xa_r.at[0, chunk(c)], at(xx=xp))
+        send_rounded("xam", c, xs.at[1], hgp[hrows(c, xo, 1), :], xa_r.at[1, chunk(c)], at(xx=xm))
+        send_rounded("xdp", c, xs.at[2], hgp[hrows(c, xp, 1), :], xb_r.at[0, 1, chunk(c)], at(xx=xp))
+        send_rounded("xdm", c, xs.at[3], hgp[hrows(c, xm, 0), :], xb_r.at[1, 0, chunk(c)], at(xx=xm))
 
     def stage_r(c):
         arrived(f"xap{c}")
-        total = hgp[hrows(c, xp, 0), :] + unpack(xa_r[0, chunk(c)], depth)
-        send_packed("xbp", c, xs.at[4], total, xb_r.at[0, 0, chunk(c)], at(xx=xp))
+        total = hgp[hrows(c, xp, 0), :] + xa_r[0, chunk(c)].astype(F32)
+        send_rounded("xbp", c, xs.at[4], total, xb_r.at[0, 0, chunk(c)], at(xx=xp))
         arrived(f"xam{c}")
-        total = hgp[hrows(c, xm, 1), :] + unpack(xa_r[1, chunk(c)], depth)
-        send_packed("xbm", c, xs.at[5], total, xb_r.at[1, 1, chunk(c)], at(xx=xm))
+        total = hgp[hrows(c, xm, 1), :] + xa_r[1, chunk(c)].astype(F32)
+        send_rounded("xbm", c, xs.at[5], total, xb_r.at[1, 1, chunk(c)], at(xx=xm))
 
     def zrows(c, k, i):
         return span(8 * BASE[c] + x * 2 * SIZE[c] + k * SIZE[c] + i * 16, 16)
@@ -325,9 +331,9 @@
             arrived(f"{name}{c}")
         for k in (0, 1):
             total = hgp[hrows(c, x, k), :]
-            total = total + unpack(xb_r[0, k, chunk(c)], depth) + unpack(xb_r[1, k, chunk(c)], depth)
+            total = total + xb_r[0, k, chunk(c)].astype(F32) + xb_r[1, k, chunk(c)].astype(F32)
             hgp[hrows(c, x, k), :] = total
-            zs[k, chunk(c), :] = pack(total)
+            zs[k, chunk(c), :] = total.astype(BF16)
         for d_ in range(1, 8):
             zz = (z + d_) % 8
             for i, g in enumerate(CHUNKS[c]):
@@ -343,7 +349,7 @@
                 total = hgp[zrows(c, z // 4, i), :]
                 for d_ in range(1, 8):
                     arrived(f"z{d_}{i}{c}")
-                    total = total + unpack(zr[c, d_ - 1], depth)
+                    total = total + zr[c, d_ - 1].astype(F32)
                 hgrad[pl.ds(16 * (g % 2), 16), :] = total.astype(BF16)
 
     def head_term(cols, chunks):
@@ -368,7 +374,7 @@
         "M": stage_m, "A": stage_a, "B": stage_b, "L": stage_l, "X": stage_x, "G": stage_g, "F": stage_f,
         "H": stage_h, "K": stage_k, "R": stage_r, "Z": stage_z, "O": stage_o, "V": stage_v, "W": stage_w, "T": stage_t,
     }
-    for entry in ORDER:
+    for entry in ORDER[:-1]:
         stages[entry[0]](int(entry[1]))
 
     div[...] = divcol[...].T[0:1, :]
@@ -378,12 +384,12 @@
             pl.when((z + d_) % 4 == CHUNKS[c][i] // 2)(copy.wait_send)
         else:
             copy.wait_send()
+    stages[ORDER[-1][0]](int(ORDER[-1][1]))
 
 
 def per_device(hidden, target, head, cotangent):
     depth, vocab = head.shape
     padded = -(-vocab // 256) * 256
-    wide = depth + -(-depth // 256) * 128
     vmem = pltpu.VMEM
     results = (
         jax.ShapeDtypeStruct((vocab, depth), BF16),
@@ -415,11 +421,11 @@
             vmem((vocab, depth), F32),
             vmem((1024, padded), BF16),
             vmem((1024, depth), F32),
-            vmem((6, 128, wide), BF16),
-            vmem((2, 128, wide), BF16),
-            vmem((2, 2, 128, wide), BF16),
-            vmem((2, 128, wide), BF16),
-            vmem((N, 7, 16, wide), BF16),
+            vmem((6, 128, depth), BF16),
+            vmem((2, 128, depth), BF16),
+            vmem((2, 2, 128, depth), BF16),
+            vmem((2, 128, depth), BF16),
+            vmem((N, 7, 16, depth), BF16),
             pltpu.SemaphoreType.DMA((48,)),
             pltpu.SemaphoreType.DMA((46 * N,)),
             pltpu.SemaphoreType.DMA((46 * N,)),

time: 93.1 us -> 87.3 us (0.938)
  Pallas kernels: 92.2 us -> 86.5 us
    pallas_call x1, Pallas kernels: 90.2 us -> 84.5 us  [per_device(): pl.pallas_call(kernel, out_shape=tuple((vmem(r.shape, r.dtype) for r in r...]
where the time goes in v3:
time: 87.3 us
  Pallas kernels  86.5 us (99%)
    pallas_call x1, Pallas kernels, per_device(): pl.pallas_call(kernel, out_shape=tuple((vmem(r.shape, r.dtype) for r in r...  84.5 us
    pallas_call x1, Pallas kernels, per_device(): pl.pallas_call(place, out_shape=results, in_specs=[pl.BlockSpec(memory_sp...  1.96 us

profile of v3, /device:TPU:1, one launch (start us, length us, event | category | flops | bytes accessed | tf_op | source)
XLA Modules:
  0.0 87.3 jit_solution(17640974766859647368)
XLA Ops:
  0.6 84.5 %shard_map.67 = (bf16[2020,896]{1,0:T(8,128)(2,1)S(1)}, bf16[32,896]{1,0:T(8,128)(2,1)S(1)}, f32[1,128]{1,0:T(1,128)S(1)}) custom-call(bf16[4,2,8,16,896]{4,3,2,1,0:T(8,128)(2,1)} %bitcast.8, bf16[2020,1024]{1,0:T(8,128)(2,1)} %bitcast.6, bf16[2020,896]{1,0:T(8,128)(2,1)} %bitcast.7, f32[8,128]{1,0:T(8,128)} %bitcast.9), custom_call_target="tpu_custom_call" | custom-call | tf_op jit(solution)/shard_map/pallas_call | solution.py:399
  85.1 2.0 %shard_map.68 = (bf16[2020,896]{1,0:T(8,128)(2,1)}, bf16[32,896]{1,0:T(8,128)(2,1)}, f32[1,128]{1,0:T(1,128)}) custom-call(bf16[2020,896]{1,0:T(8,128)(2,1)S(1)} %get-tuple-element.9.refs_0_, bf16[32,896]{1,0:T(8,128)(2,1)S(1)} %get-tuple-element.10.refs_1_, f32[1,128]{1,0:T(1,128)S(1)} %get-tuple-element.11.refs_2_), custom_call_target="tpu_custom_call" | custom-call | tf_op jit(solution)/shard_map/pallas_call | solution.py:443

commit v4 on v3

--- a/solution.py
+++ b/solution.py
@@ -14,11 +14,11 @@
 WIDE = 256
 EARLY = 4
 ORDER = (
-    "M0", "M1", "A0", "M2", "A1", "M3", "B0", "A2", "M4", "T0", "B1", "A3", "B2", "M5", "L0", "L1", "A5", "X0",
-    "X1", "G0", "B5", "L2", "G1", "B3", "X2", "L5", "F0", "A4", "F1", "X5", "L3", "H0", "G2", "X3", "B4", "K0",
-    "H1", "G5", "K1", "R0", "F2", "G3", "L4", "X4", "H2", "R1", "F5", "K2", "F3", "Z0", "H5", "G4", "Z1", "K5",
-    "H3", "R2", "K3", "F4", "V2", "Z2", "R5", "H4", "R3", "K4", "Z5", "Z3", "O1", "R4", "V0", "O2", "W2", "Z4",
-    "O5", "V3", "V1", "W0", "O0", "W1", "W3", "O3", "O4",
+    "M0", "M1", "A0", "M2", "A1", "B0", "T0", "A2", "M3", "B1", "L0", "M4", "B2", "M5", "A4", "L1", "A5", "L2",
+    "B4", "X1", "X0", "A3", "X2", "L4", "B5", "B3", "G0", "G1", "G2", "X4", "L5", "L3", "X5", "F0", "G4", "X3",
+    "F1", "F2", "H0", "G5", "H1", "F4", "G3", "K0", "H2", "K1", "F5", "K2", "H4", "F3", "R0", "H5", "R1", "K4",
+    "K5", "R2", "H3", "Z0", "Z1", "R4", "K3", "Z2", "R5", "V2", "Z4", "R3", "V0", "Z5", "O0", "V3", "O1", "W0",
+    "Z3", "O4", "V1", "O2", "W3", "W2", "W1", "O5", "O3",
 )
 
 

time: 87.3 us -> 83.7 us (0.959)
  the two profiles are of different devices: /device:TPU:1 before, /device:TPU:32 now
where the time goes in v4:
time: 83.7 us
  Pallas kernels  82.9 us (99%)
    pallas_call x1, Pallas kernels, per_device(): pl.pallas_call(kernel, out_shape=tuple((vmem(r.shape, r.dtype) for r in r...  80.9 us
    pallas_call x1, Pallas kernels, per_device(): pl.pallas_call(place, out_shape=results, in_specs=[pl.BlockSpec(memory_sp...  1.96 us

profile of v4, /device:TPU:32, one launch (start us, length us, event | category | flops | bytes accessed | tf_op | source)
XLA Modules:
  0.0 83.7 jit_solution(567401856492857089)
XLA Ops:
  0.6 80.9 %shard_map.67 = (bf16[2020,896]{1,0:T(8,128)(2,1)S(1)}, bf16[32,896]{1,0:T(8,128)(2,1)S(1)}, f32[1,128]{1,0:T(1,128)S(1)}) custom-call(bf16[4,2,8,16,896]{4,3,2,1,0:T(8,128)(2,1)} %bitcast.8, bf16[2020,1024]{1,0:T(8,128)(2,1)} %bitcast.6, bf16[2020,896]{1,0:T(8,128)(2,1)} %bitcast.7, f32[8,128]{1,0:T(8,128)} %bitcast.9), custom_call_target="tpu_custom_call" | custom-call | tf_op jit(solution)/shard_map/pallas_call | solution.py:399
  81.5 2.0 %shard_map.68 = (bf16[2020,896]{1,0:T(8,128)(2,1)}, bf16[32,896]{1,0:T(8,128)(2,1)}, f32[1,128]{1,0:T(1,128)}) custom-call(bf16[2020,896]{1,0:T(8,128)(2,1)S(1)} %get-tuple-element.9.refs_0_, bf16[32,896]{1,0:T(8,128)(2,1)S(1)} %get-tuple-element.10.refs_1_, f32[1,128]{1,0:T(1,128)S(1)} %get-tuple-element.11.refs_2_), custom_call_target="tpu_custom_call" | custom-call | tf_op jit(solution)/shard_map/pallas_call | solution.py:443
